TPU v7x, 32 devices: a whole 2x2x4 slice. The times are simulated.
32 devices in a mesh: slab: 4 (over y, x), box: 8 (over z, core).
Axes of the slice: x: 2, y: 2, z: 4, core: 2. Of those that a mesh axis runs over, the one named last changes fastest.
Arguments:
- currents: bfloat16 [256, 128, 128], P(('slab', 'box')), may hold values from -6 to 6
- aggregate: bfloat16 [2, 512, 128], replicated, may hold values from -0.5 to 0.5
- disaggregate: bfloat16 [128, 2, 512], replicated, may hold values from -0.1875 to 0.1875
- trans_table: float32 [316, 2, 512], replicated, may hold values from -3 to 3
- trans_src: int32 [256, 4], P('slab'), may hold values from 0 to 63
- trans_kind: int32 [256, 4], P('slab'), may hold values from 0 to 315
- near_blocks: bfloat16 [27, 128, 128], replicated, may hold values from -0.109375 to 0.109375
- near_src: int32 [256, 27], P(('slab', 'box')), may hold values from 0 to 23
- near_kind: int32 [256, 27], P(('slab', 'box')), may hold values from 0 to 26
Outputs:
- field: float32 [256, 128, 128], P(('slab', 'box'))
All inputs are finite; a program needn't handle non-finite values.
Results may differ from a plain program's by a relative error of at most 0.0035.
Values may be sent and summed in bfloat16 or wider, within the bound.
A program may use at most 64 MiB of HBM per device.

v0:
```python
import jax
import jax.numpy as jnp
from jax import lax
from jax.sharding import PartitionSpec as P


def with_halo(block, sides, width):
    for axis, dim in sides:
        count = lax.axis_size(axis)
        forward = [(i, i + 1) for i in range(count - 1)]
        backward = [(target, source) for source, target in forward]
        low = lax.ppermute(
            lax.slice_in_dim(block, block.shape[dim] - width, None, axis=dim), axis, forward
        )
        high = lax.ppermute(lax.slice_in_dim(block, 0, width, axis=dim), axis, backward)
        block = jnp.concatenate([low, block, high], axis=dim)
    return block


def translate(pattern, coeffs, sources, kinds):
    real_part = None
    imag_part = None
    for entry in range(sources.shape[1]):
        source = pattern[sources[:, entry]].astype(jnp.float32)
        chosen = coeffs[kinds[:, entry]]
        coef_real = chosen[:, 0, :, None]
        coef_imag = chosen[:, 1, :, None]
        new_real = coef_real * source[:, 0] - coef_imag * source[:, 1]
        new_imag = coef_real * source[:, 1] + coef_imag * source[:, 0]
        if real_part is None:
            real_part = new_real
            imag_part = new_imag
        else:
            real_part = real_part + new_real
            imag_part = imag_part + new_imag
    return jnp.stack([real_part, imag_part], 1).astype(jnp.bfloat16)


def on_device(
    currents,
    aggregate,
    disaggregate,
    trans_table,
    trans_src,
    trans_kind,
    near_blocks,
    near_src,
    near_kind,
):
    box_dev = currents.shape[0]
    box_count = lax.axis_size("box")
    per_device = trans_table.shape[2] // box_count
    pattern = jnp.einsum(
        "cdu,bue->bcde", aggregate, currents, preferred_element_type=jnp.float32
    ).astype(jnp.bfloat16)
    by_direction = lax.all_to_all(pattern, "box", split_axis=2, concat_axis=0, tiled=True)
    coeffs = lax.dynamic_slice_in_dim(
        trans_table, lax.axis_index("box") * per_device, per_device, 2
    )
    incoming = translate(by_direction, coeffs, trans_src, trans_kind)
    returned = lax.all_to_all(incoming, "box", split_axis=0, concat_axis=2, tiled=True)
    far = jnp.einsum("ucd,bcde->bue", disaggregate, returned, preferred_element_type=jnp.float32)
    extended = with_halo(currents, (("slab", 0),), box_dev)
    cand_ids = jnp.arange(extended.shape[0], dtype=jnp.int32)
    pick_src = (near_src[:, :, None] == cand_ids[None, None, :]).astype(jnp.bfloat16)
    kind_ids = jnp.arange(near_blocks.shape[0], dtype=jnp.int32)
    pick_kind = (near_kind[:, :, None] == kind_ids[None, None, :]).astype(jnp.bfloat16)
    sources = jnp.einsum(
        "blk,kve->blve", pick_src, extended, preferred_element_type=jnp.float32
    ).astype(jnp.bfloat16)
    blocks = jnp.einsum(
        "blk,kuv->bulv", pick_kind, near_blocks, preferred_element_type=jnp.float32
    ).astype(jnp.bfloat16)
    near = jnp.einsum("bulv,blve->bue", blocks, sources, preferred_element_type=jnp.float32)
    return near + far


def solution(mesh):
    placed = (
        P(("slab", "box"), None, None),
        P(),
        P(),
        P(),
        P("slab", None),
        P("slab", None),
        P(),
        P(("slab", "box"), None),
        P(("slab", "box"), None),
    )
    return jax.shard_map(
        on_device,
        mesh=mesh,
        in_specs=placed,
        out_specs=P(("slab", "box"), None, None),
        check_vma=False,
    )
```

profile of v0, /device:TPU:1, one launch (start us, length us, event | category | flops | bytes accessed | tf_op | source)
XLA Modules:
  0.0 166.4 jit_solution(969948816888774342)
XLA Ops:
  0.0 1.9 %convert_bitcast_fusion.1 = bf16[8,2,512,128]{2,3,1,0:T(8,128)(2,1)S(1)} fusion(bf16[8,128,128]{2,1,0:T(8,128)(2,1)} %param.9, bf16[2,512,128]{2,1,0:T(8,128)(2,1)} %param.10), kind=kOutput, calls=%fused_computation.16 | convolution fusion | flops 269484032 | bytes 2621440 | tf_op jit(solution)/shard_map/cdu,bue->bcde/dot_general | solution.py:53
  1.9 4.1 %copy.27 = bf16[8,2,512,128]{3,1,0,2:T(2,128)(2,1)} copy(bf16[8,2,512,128]{2,3,1,0:T(8,128)(2,1)S(1)} %convert_bitcast_fusion.1) | data formatting | bytes 4194304 | tf_op jit(solution)/shard_map/convert_element_type | solution.py:55
  5.9 6.5 %all-to-all-start = ((bf16[8,2,512,128]{3,1,0,2:T(2,128)(2,1)}), bf16[8,2,512,128]{3,1,0,2:T(2,128)(2,1)S(1)}, u32[]{:S(2)}, u32[]{:S(2)}) async-start(bf16[8,2,512,128]{3,1,0,2:T(2,128)(2,1)} %copy.27), calls=%async_computation | async-start | bytes 4194304 | tf_op jit(solution)/shard_map/all_to_all | solution.py:56
  12.5 1.1 constant_dynamic-slice_fusion
  13.6 1.6 gather_fusion
  15.2 2.2 %gather_fusion.2 = f32[64,2,64]{2,1,0:T(2,128)} fusion(f32[316,2,64]{2,1,0:T(2,128)} %constant_dynamic-slice_fusion, s32[1024]{0:T(1024)S(1)} %get-tuple-element.23), kind=kCustom, calls=%fused_computation.2 | custom fusion | bytes 65792 | tf_op jit(solution)/shard_map/gather | solution.py:25
  17.5 2.2 %gather_fusion.4 = f32[64,2,64]{2,1,0:T(2,128)} fusion(f32[316,2,64]{2,1,0:T(2,128)} %constant_dynamic-slice_fusion, s32[1024]{0:T(1024)S(1)} %get-tuple-element.22), kind=kCustom, calls=%fused_computation.4 | custom fusion | bytes 65792 | tf_op jit(solution)/shard_map/gather | solution.py:25
  19.7 2.2 %gather_fusion.6 = f32[64,2,64]{2,1,0:T(2,128)} fusion(f32[316,2,64]{2,1,0:T(2,128)} %constant_dynamic-slice_fusion, s32[1024]{0:T(1024)S(1)} %get-tuple-element.21), kind=kCustom, calls=%fused_computation.6 | custom fusion | bytes 65792 | tf_op jit(solution)/shard_map/gather | solution.py:25
  23.2 1.0 fusion.39
  24.2 1.6 fusion.40
  25.8 1.6 fusion.41
  27.4 33.3 %all-to-all-done = bf16[8,2,512,128]{3,1,0,2:T(2,128)(2,1)S(1)} async-done(((bf16[8,2,512,128]{3,1,0,2:T(2,128)(2,1)}), bf16[8,2,512,128]{3,1,0,2:T(2,128)(2,1)S(1)}, u32[]{:S(2)}, u32[]{:S(2)}) %all-to-all-start) | async-done | bytes 2097184 | tf_op jit(solution)/shard_map/all_to_all | solution.py:56
  61.4 2.3 %gather_fusion.1 = bf16[64,2,64,128]{3,2,1,0:T(8,128)(2,1)} fusion(bf16[64,2,64,128]{3,2,1,0:T(8,128)(2,1)S(1)} %bitcast.73, s32[1024]{0:T(1024)} %get-tuple-element.28), kind=kCustom, calls=%fused_computation.1 | custom fusion | bytes 4194560 | tf_op jit(solution)/shard_map/gather | solution.py:24
  63.7 4.0 %convert_element_type.35 = f32[64,2,64,128]{3,2,1,0:T(8,128)} convert(bf16[64,2,64,128]{3,2,1,0:T(8,128)(2,1)} %gather_fusion.1) | non-fusion elementwise | flops 1048576 | bytes 6291456 | tf_op jit(solution)/shard_map/convert_element_type | solution.py:24
  67.7 2.3 %gather_fusion.3 = bf16[64,2,64,128]{3,2,1,0:T(8,128)(2,1)} fusion(bf16[64,2,64,128]{3,2,1,0:T(8,128)(2,1)S(1)} %bitcast.74, s32[1024]{0:T(1024)} %get-tuple-element.27), kind=kCustom, calls=%fused_computation.3 | custom fusion | bytes 4194560 | tf_op jit(solution)/shard_map/gather | solution.py:24
  70.0 4.1 %convert_element_type.36 = f32[64,2,64,128]{3,2,1,0:T(8,128)} convert(bf16[64,2,64,128]{3,2,1,0:T(8,128)(2,1)} %gather_fusion.3) | non-fusion elementwise | flops 1048576 | bytes 6291456 | tf_op jit(solution)/shard_map/convert_element_type | solution.py:24
  74.2 2.2 %gather_fusion.5 = bf16[64,2,64,128]{3,2,1,0:T(8,128)(2,1)} fusion(bf16[64,2,64,128]{3,2,1,0:T(8,128)(2,1)S(1)} %bitcast.75, s32[1024]{0:T(1024)} %get-tuple-element.26), kind=kCustom, calls=%fused_computation.5 | custom fusion | bytes 4194560 | tf_op jit(solution)/shard_map/gather | solution.py:24
  76.4 4.1 %convert_element_type.37 = f32[64,2,64,128]{3,2,1,0:T(8,128)} convert(bf16[64,2,64,128]{3,2,1,0:T(8,128)(2,1)} %gather_fusion.5) | non-fusion elementwise | flops 1048576 | bytes 6291456 | tf_op jit(solution)/shard_map/convert_element_type | solution.py:24
  80.5 2.2 %gather_fusion.7 = bf16[64,2,64,128]{3,2,1,0:T(8,128)(2,1)} fusion(bf16[64,2,64,128]{3,2,1,0:T(8,128)(2,1)S(1)} %bitcast.76, s32[1024]{0:T(1024)} %get-tuple-element.25), kind=kCustom, calls=%fused_computation.7 | custom fusion | bytes 4194560 | tf_op jit(solution)/shard_map/gather | solution.py:24
  82.7 2.2 %convert_element_type.38 = f32[64,2,64,128]{3,2,1,0:T(8,128)S(1)} convert(bf16[64,2,64,128]{3,2,1,0:T(8,128)(2,1)} %gather_fusion.7) | non-fusion elementwise | flops 1048576 | bytes 6291456 | tf_op jit(solution)/shard_map/convert_element_type | solution.py:24
  85.6 9.0 %add_convert_fusion.1 = bf16[64,1,64,128]{3,2,1,0:T(8,128)(2,1)S(1)} fusion(f32[64,2,64,128]{3,2,1,0:T(8,128)S(1)} %convert_element_type.38, f32[64,2,64,128]{3,2,1,0:T(8,128)} %convert_element_type.37, f32[64,2,64,128]{3,2,1,0:T(8,128)} %convert_element_type.36, f32[64,2,64,128]{3,2,1,0:T(8,128)S(1)} %copy-done.1, f32[64,64]{1,0:T(8,128)S(1)} %bitcast.94, ...), kind=kLoop, calls=%fused_computation.15 | loop fusion | flops 8388608 | bytes 17956864 | tf_op jit(solution)/shard_map/convert
  94.6 5.0 %add_convert_fusion = bf16[64,1,64,128]{3,2,1,0:T(8,128)(2,1)S(1)} fusion(f32[64,2,64,128]{3,2,1,0:T(8,128)S(1)} %convert_element_type.38, f32[64,2,64,128]{3,2,1,0:T(8,128)S(1)} %copy-done.3, f32[64,2,64,128]{3,2,1,0:T(8,128)S(1)} %copy-done.2, f32[64,2,64,128]{3,2,1,0:T(8,128)S(1)} %copy-done.1, f32[64,64]{1,0:T(8,128)S(1)} %bitcast.95, ...), kind=kLoop, calls=%fused_computation.14 | loop fusion | flops 8388608 | bytes 17956864 | tf_op jit(solution)/shard_map/convert.1
  99.6 1.5 pad_maximum_fusion
  101.1 4.5 %all-to-all-start.1 = ((bf16[64,2,64,128]{3,2,1,0:T(8,128)(2,1)}), bf16[64,2,64,128]{3,2,1,0:T(8,128)(2,1)S(1)}, u32[]{:S(2)}, u32[]{:S(2)}) async-start(bf16[64,2,64,128]{3,2,1,0:T(8,128)(2,1)} %pad_maximum_fusion), calls=%async_computation.1 | async-start | bytes 4194304 | tf_op jit(solution)/shard_map/all_to_all | solution.py:61
  105.6 1.1 copy.21
  106.8 3.2 %collective-permute-start = (bf16[8,128,128]{2,0,1:T(8,128)(2,1)S(1)}, bf16[8,128,128]{2,0,1:T(8,128)(2,1)S(1)}, u32[]{:S(2)}, u32[]{:S(2)}) collective-permute-start(bf16[8,128,128]{2,0,1:T(8,128)(2,1)S(1)} %copy.21), channel_id=1, source_target_pairs={{0,8},{8,16},{16,24},{1,9},{9,17},{17,25},{2,10},{10,18},{18,26},{... | collective-permute-start | bytes 786440 | tf_op jit(solution)/shard_map/ppermute | solution.py:12
  109.9 1.5 collective-permute-start.1
  111.4 6.8 %convert_bitcast_fusion = bf16[8,128,27,128]{3,2,1,0:T(8,128)(2,1)} fusion(bf16[27,128,128]{2,1,0:T(8,128)(2,1)} %param.15, s32[8,27]{1,0:T(8,128)S(1)} %copy-done.8), kind=kOutput, calls=%fused_computation.8 | convolution fusion | flops 194647744 | bytes 7963488 | tf_op jit(solution)/shard_map/blk,kuv->bulv/dot_general | solution.py:71
  118.2 4.9 %collective-permute-done.1 = bf16[8,128,128]{2,0,1:T(8,128)(2,1)S(1)} collective-permute-done((bf16[8,128,128]{2,0,1:T(8,128)(2,1)S(1)}, bf16[8,128,128]{2,0,1:T(8,128)(2,1)S(1)}, u32[]{:S(2)}, u32[]{:S(2)}) %collective-permute-start.1) | collective-permute-done | bytes 262176 | tf_op jit(solution)/shard_map/ppermute | solution.py:15
  123.1 4.6 %convolution_convert_fusion = bf16[8,27,128,128]{3,1,2,0:T(8,128)(2,1)} fusion(bf16[8,128,128]{2,0,1:T(8,128)(2,1)S(1)} %collective-permute-done.1, bf16[8,128,128]{2,0,1:T(8,128)(2,1)S(1)} %copy.21, bf16[8,128,128]{2,0,1:T(8,128)(2,1)S(1)} %collective-permute-done, s32[8,27]{1,0:T(8,128)S(1)} %copy-done.9), kind=kOutput, calls=%fused_computation.12 | convolution fusion | flops 175772736 | bytes 7865184 | tf_op jit(solution)/shard_map/blk,kve->blve/dot_general | solution.py:68
  127.7 26.1 %all-to-all-done.1 = bf16[64,2,64,128]{3,2,1,0:T(8,128)(2,1)S(1)} async-done(((bf16[64,2,64,128]{3,2,1,0:T(8,128)(2,1)}), bf16[64,2,64,128]{3,2,1,0:T(8,128)(2,1)S(1)}, u32[]{:S(2)}, u32[]{:S(2)}) %all-to-all-start.1) | async-done | bytes 2097184 | tf_op jit(solution)/shard_map/all_to_all | solution.py:61
  155.2 11.2 %fusion.8 = f32[8,128,128]{2,1,0:T(8,128)} fusion(f32[8,128,128]{2,1,0:T(8,128)S(1)} %convolution_bitcast_fusion, bf16[8,27,128,128]{3,1,2,0:T(8,128)(2,1)} %convolution_convert_fusion, bf16[8,128,27,128]{3,2,1,0:T(8,128)(2,1)} %convert_bitcast_fusion), kind=kOutput, calls=%fused_computation.19 | convolution fusion | flops 906100736 | bytes 15204352 | tf_op jit(solution)/shard_map/bulv,blve->bue/dot_general | solution.py:74
  (36 shorter events, 4.0 us)
Async XLA Ops:
  0.0 12.5 %copy-start = (f32[316,2,512]{2,1,0:T(2,128)S(1)}, f32[316,2,512]{2,1,0:T(2,128)}, u32[]{:S(2)}) copy-start(f32[316,2,512]{2,1,0:T(2,128)} %param.12) | copy-start | bytes 3883012
  5.9 6.5 %copy-start.10 = (s32[64,4]{0,1:T(4,128)S(1)}, s32[64,4]{0,1:T(4,128)}, u32[]{:S(2)}) copy-start(s32[64,4]{0,1:T(4,128)} %param.14) | copy-start | bytes 3076
  5.9 16.0 %copy-start.11 = (s32[64,4]{0,1:T(4,128)S(1)}, s32[64,4]{0,1:T(4,128)}, u32[]{:S(2)}) copy-start(s32[64,4]{0,1:T(4,128)} %param.13) | copy-start | bytes 3076
  5.9 54.7 %all-to-all-start = ((bf16[8,2,512,128]{3,1,0,2:T(2,128)(2,1)}), bf16[8,2,512,128]{3,1,0,2:T(2,128)(2,1)S(1)}, u32[]{:S(2)}, u32[]{:S(2)}) async-start(bf16[8,2,512,128]{3,1,0,2:T(2,128)(2,1)} %copy.27), calls=%async_computation | async-start | bytes 4194304 | tf_op jit(solution)/shard_map/all_to_all | solution.py:56
  82.7 2.8 %copy-start.1 = (f32[64,2,64,128]{3,2,1,0:T(8,128)S(1)}, f32[64,2,64,128]{3,2,1,0:T(8,128)}, u32[]{:S(2)}) copy-start(f32[64,2,64,128]{3,2,1,0:T(8,128)} %convert_element_type.35) | copy-start | bytes 12582916
  82.7 2.8 %copy-start.4 = (f32[64,1,64]{2,1,0:T(1,128)S(1)}, f32[64,1,64]{2,1,0:T(1,128)}, u32[]{:S(2)}) copy-start(f32[64,1,64]{2,1,0:T(1,128)} %get-tuple-element.10) | copy-start | bytes 49156
  82.7 2.8 %copy-start.5 = (f32[64,1,64]{2,1,0:T(1,128)S(1)}, f32[64,1,64]{2,1,0:T(1,128)}, u32[]{:S(2)}) copy-start(f32[64,1,64]{2,1,0:T(1,128)} %get-tuple-element.11) | copy-start | bytes 49156
  82.7 2.8 %copy-start.6 = (f32[64,1,64]{2,1,0:T(1,128)S(1)}, f32[64,1,64]{2,1,0:T(1,128)}, u32[]{:S(2)}) copy-start(f32[64,1,64]{2,1,0:T(1,128)} %get-tuple-element.12) | copy-start | bytes 49156
  85.5 9.0 %copy-start.2 = (f32[64,2,64,128]{3,2,1,0:T(8,128)S(1)}, f32[64,2,64,128]{3,2,1,0:T(8,128)}, u32[]{:S(2)}) copy-start(f32[64,2,64,128]{3,2,1,0:T(8,128)} %convert_element_type.36) | copy-start | bytes 12582916
  85.5 9.0 %copy-start.3 = (f32[64,2,64,128]{3,2,1,0:T(8,128)S(1)}, f32[64,2,64,128]{3,2,1,0:T(8,128)}, u32[]{:S(2)}) copy-start(f32[64,2,64,128]{3,2,1,0:T(8,128)} %convert_element_type.37) | copy-start | bytes 12582916
  101.1 10.3 %copy-start.8 = (s32[8,27]{1,0:T(8,128)S(1)}, s32[8,27]{1,0:T(8,128)}, u32[]{:S(2)}) copy-start(s32[8,27]{1,0:T(8,128)} %param.17) | copy-start | bytes 2596
  101.1 52.7 %all-to-all-start.1 = ((bf16[64,2,64,128]{3,2,1,0:T(8,128)(2,1)}), bf16[64,2,64,128]{3,2,1,0:T(8,128)(2,1)S(1)}, u32[]{:S(2)}, u32[]{:S(2)}) async-start(bf16[64,2,64,128]{3,2,1,0:T(8,128)(2,1)} %pad_maximum_fusion), calls=%async_computation.1 | async-start | bytes 4194304 | tf_op jit(solution)/shard_map/all_to_all | solution.py:61
  106.7 16.4 %copy-start.9 = (s32[8,27]{1,0:T(8,128)S(1)}, s32[8,27]{1,0:T(8,128)}, u32[]{:S(2)}) copy-start(s32[8,27]{1,0:T(8,128)} %param.16) | copy-start | bytes 2596
  106.8 11.4 %collective-permute-start = (bf16[8,128,128]{2,0,1:T(8,128)(2,1)S(1)}, bf16[8,128,128]{2,0,1:T(8,128)(2,1)S(1)}, u32[]{:S(2)}, u32[]{:S(2)}) collective-permute-start(bf16[8,128,128]{2,0,1:T(8,128)(2,1)S(1)} %copy.21), channel_id=1, source_target_pairs={{0,8},{8,16},{16,24},{1,9},{9,17},{17,25},{2,10},{10,18},{18,26},{... | collective-permute-start | bytes 786440 | tf_op jit(solution)/shard_map/ppermute | solution.py:12
  109.9 13.2 %collective-permute-start.1 = (bf16[8,128,128]{2,0,1:T(8,128)(2,1)S(1)}, bf16[8,128,128]{2,0,1:T(8,128)(2,1)S(1)}, u32[]{:S(2)}, u32[]{:S(2)}) collective-permute-start(bf16[8,128,128]{2,0,1:T(8,128)(2,1)S(1)} %copy.21), channel_id=1, source_target_pairs={{8,0},{16,8},{24,16},{9,1},{17,9},{25,17},{10,2},{18,10},{26,18},{... | collective-permute-start | bytes 786440 | tf_op jit(solution)/shard_map/ppermute | solution.py:15
  153.8 1.0 copy-start.7
where the time goes:
time: 168 us; the launch traced here: 166 us
  waiting for transfers between devices  64.3 us (38%)
  other arithmetic  31.2 us (19%)
  local copies, waits for them, and re-layouts  30.2 us (18%)
  matrix products  24.8 us (15%)
  starting transfers between devices  15.6 us (9%)
    all_to_all x1, waiting for transfers between devices, on_device(): lax.all_to_all(pattern, 'box', split_axis=2, concat_axis=0, tiled=True)  33.3 us
    all_to_all x1, waiting for transfers between devices, on_device(): lax.all_to_all(incoming, 'box', split_axis=0, concat_axis=2, tiled=True)  26.1 us
    convert_element_type x4, other arithmetic, translate(): source = pattern[sources[:, entry]].astype(jnp.float32)  14.5 us
    another operation x2, other arithmetic  14 us
    dot_general x1, matrix products, on_device(): jnp.einsum('bulv,blve->bue', blocks, sources, preferred_element_type=jnp....  11.2 us
    gather x4, local copies, waits for them, and re-layouts, translate(): source = pattern[sources[:, entry]].astype(jnp.float32)  9.1 us
    gather x4, local copies, waits for them, and re-layouts, translate(): chosen = coeffs[kinds[:, entry]]  8.32 us
    dot_general x1, matrix products, on_device(): jnp.einsum('blk,kuv->bulv', pick_kind, near_blocks, preferred_element_typ...  6.77 us
  transfers between devices with their start and end apart: 4, of which 3 were waited for; matrix products, arithmetic and copies ran while one was open for 16% of the time, Pallas kernels for 0%

commit v1 on v0

v1 whole, which is shorter than its diff:
```python
import functools

import jax
import jax.numpy as jnp
from jax import lax
from jax.experimental import pallas as pl
from jax.experimental.pallas import tpu as pltpu
from jax.sharding import PartitionSpec as P

MESH = pl.DeviceIdType.MESH
CHUNKS = 2


def spread(total, parts):
    return [total * i // parts for i in range(parts + 1)]


def kernel(
    n_slab,
    n_box,
    trans_src,
    trans_kind,
    near_src,
    near_kind,
    currents,
    aggregate,
    disaggregate,
    trans_table,
    near_blocks,
    out,
    gathered,
    cand,
    agg,
    dis,
    dis_wide,
    table,
    blocks,
    weights,
    operators,
    load_sem,
    halo_send,
    halo_recv,
    own_send,
    line_send,
    line_recv,
    pair_send,
    pair_recv,
):
    slab = lax.axis_index("slab")
    box = lax.axis_index("box")
    place = box // 2
    core = box % 2
    chips = n_box // 2
    n_own, unk, exc = currents.shape
    per = n_own // CHUNKS
    dirs = agg.shape[1]
    n_trans = trans_src.shape[0]
    n_near = near_src.shape[1]

    def peer(slab_step, box_id):
        return (slab + slab_step, box_id)

    pair_id = place * 2 + (1 - core)
    neighbours = [
        (place > 0, peer(0, box - 2)),
        (place < chips - 1, peer(0, box + 2)),
        (None, peer(0, pair_id)),
        (slab > 0, peer(-1, box)),
        (slab < n_slab - 1, peer(1, box)),
    ]

    def when(cond):
        return (lambda f: f()) if cond is None else pl.when(cond)

    own = pl.ds(box * n_own, n_own)
    loads = [
        pltpu.make_async_copy(currents, gathered.at[own], load_sem.at[0]),
        pltpu.make_async_copy(currents, cand.at[pl.ds(n_own, n_own)], load_sem.at[1]),
        pltpu.make_async_copy(disaggregate, dis, load_sem.at[2]),
        pltpu.make_async_copy(trans_table, table, load_sem.at[3]),
        pltpu.make_async_copy(aggregate, agg, load_sem.at[4]),
        pltpu.make_async_copy(near_blocks, blocks, load_sem.at[5]),
    ]
    for load in loads:
        load.start()

    barrier = pltpu.get_barrier_semaphore()
    for cond, target in neighbours:
        @when(cond)
        def _():
            pl.semaphore_signal(barrier, inc=1, device_id=target, device_id_type=MESH)
    met = (
        1
        + (place > 0).astype(jnp.int32)
        + (place < chips - 1).astype(jnp.int32)
        + (slab > 0).astype(jnp.int32)
        + (slab < n_slab - 1).astype(jnp.int32)
    )
    pl.semaphore_wait(barrier, met)

    def part(origin, lane, chunk):
        return gathered.at[pl.ds((origin * 2 + lane) * n_own + chunk * per, per)]

    def line_copy(origin, chunk, target, send):
        return pltpu.make_async_remote_copy(
            src_ref=part(origin, core, chunk),
            dst_ref=part(origin, core, chunk),
            send_sem=send,
            recv_sem=line_recv.at[origin, chunk],
            device_id=peer(0, target),
            device_id_type=MESH,
        )

    def pair_copy(origin, lane, chunk):
        return pltpu.make_async_remote_copy(
            src_ref=part(origin, lane, chunk),
            dst_ref=part(origin, lane, chunk),
            send_sem=pair_send.at[origin, chunk],
            recv_sem=pair_recv.at[origin, chunk],
            device_id=peer(0, pair_id),
            device_id_type=MESH,
        )

    def halo_copy(side):
        return pltpu.make_async_remote_copy(
            src_ref=cand.at[pl.ds(n_own, n_own)],
            dst_ref=cand.at[pl.ds(2 * n_own * side, n_own)],
            send_sem=halo_send.at[side],
            recv_sem=halo_recv.at[side],
            device_id=peer(1 - 2 * side, box),
            device_id_type=MESH,
        )

    loads[0].wait()
    for chunk in range(CHUNKS):
        @pl.when(place < chips - 1)
        def _():
            line_copy(place, chunk, box + 2, own_send.at[0, chunk]).start()

        @pl.when(place > 0)
        def _():
            line_copy(place, chunk, box - 2, own_send.at[1, chunk]).start()

    loads[1].wait()

    @pl.when(slab < n_slab - 1)
    def _():
        halo_copy(0).start()

    @pl.when(slab > 0)
    def _():
        halo_copy(1).start()

    for chunk in range(CHUNKS):
        pair_copy(place, core, chunk).start()

    @pl.when(slab == 0)
    def _():
        cand[pl.ds(0, n_own)] = jnp.zeros((n_own, unk, exc), cand.dtype)

    @pl.when(slab == n_slab - 1)
    def _():
        cand[pl.ds(2 * n_own, n_own)] = jnp.zeros((n_own, unk, exc), cand.dtype)

    loads[2].wait()
    dis_wide[0] = dis[:, 0, :].astype(jnp.float32)
    dis_wide[1] = dis[:, 1, :].astype(jnp.float32)
    loads[3].wait()
    loads[4].wait()

    rows = 32

    def operator_unit(b, carry):
        for entry in range(n_trans):
            coef = table[trans_kind[entry, box * n_own + b]]
            coef_real = coef[0:1]
            coef_imag = coef[1:2]
            for r in range(0, unk, rows):
                dis_real = dis_wide[0, r : r + rows]
                dis_imag = dis_wide[1, r : r + rows]
                at = pl.ds(entry * unk + r, rows)
                weights[at, 0:dirs] = (dis_real * coef_real + dis_imag * coef_imag).astype(
                    jnp.bfloat16
                )
                weights[at, dirs : 2 * dirs] = (
                    dis_imag * coef_real - dis_real * coef_imag
                ).astype(jnp.bfloat16)
        product = jnp.dot(
            weights[...],
            agg[...].reshape(2 * dirs, unk),
            preferred_element_type=jnp.float32,
        )
        high = product.astype(jnp.bfloat16)
        low = (product - high.astype(jnp.float32)).astype(jnp.bfloat16)
        for entry in range(n_trans):
            columns = pl.ds(entry * unk, unk)
            operators[b, 0:unk, columns] = high[entry * unk : (entry + 1) * unk]
            operators[b, unk : 2 * unk, columns] = low[entry * unk : (entry + 1) * unk]
        return carry

    def near_unit(b, carry):
        lhs = jnp.concatenate([blocks[near_kind[b, i]] for i in range(n_near)], axis=1)
        rhs = jnp.concatenate([cand[near_src[b, i]] for i in range(n_near)], axis=0)
        out[b] = jnp.dot(lhs, rhs, preferred_element_type=jnp.float32)
        return carry

    def far_unit(b, carry):
        rhs = jnp.concatenate(
            [gathered[trans_src[i, box * n_own + b]] for i in range(n_trans)], axis=0
        )
        both = jnp.dot(operators[b], rhs, preferred_element_type=jnp.float32)
        out[b] = out[b] + (both[0:unk] + both[unk:])
        return carry

    def forward(step, chunk):
        from_low = place - step
        from_high = place + step

        @pl.when(from_low >= 0)
        def _():
            line_copy(from_low, chunk, box, own_send.at[0, chunk]).wait_recv()

            @pl.when(place < chips - 1)
            def _():
                line_copy(from_low, chunk, box + 2, line_send.at[from_low, chunk]).start()

            pair_copy(from_low, core, chunk).start()

        @pl.when(from_high < chips)
        def _():
            line_copy(from_high, chunk, box, own_send.at[1, chunk]).wait_recv()

            @pl.when(place > 0)
            def _():
                line_copy(from_high, chunk, box - 2, line_send.at[from_high, chunk]).start()

            pair_copy(from_high, core, chunk).start()

    def halo_wait():
        @pl.when(slab > 0)
        def _():
            halo_copy(0).wait_recv()

        @pl.when(slab < n_slab - 1)
        def _():
            halo_copy(1).wait_recv()

    events = [(step, chunk) for step in range(1, chips) for chunk in range(CHUNKS)]
    cuts = spread(2 * n_own, len(events))
    halo_done = False
    for number, (step, chunk) in enumerate(events):
        lo, hi = cuts[number], cuts[number + 1]
        if lo < min(hi, n_own):
            lax.fori_loop(lo, min(hi, n_own), operator_unit, 0)
        if hi > n_own:
            if not halo_done:
                halo_wait()
                loads[5].wait()
                halo_done = True
            lax.fori_loop(max(lo, n_own) - n_own, hi - n_own, near_unit, 0)
        forward(step, chunk)

    for origin in range(chips):
        for chunk in range(CHUNKS):
            pair_copy(origin, 1 - core, chunk).wait_recv()

    lax.fori_loop(0, n_own, far_unit, 0)

    for origin in range(chips):
        for chunk in range(CHUNKS):
            pair_copy(origin, core, chunk).wait_send()

            @pl.when(((origin < place) & (place < chips - 1)) | ((origin > place) & (place > 0)))
            def _():
                line_copy(origin, chunk, box, line_send.at[origin, chunk]).wait_send()

    for chunk in range(CHUNKS):
        @pl.when(place < chips - 1)
        def _():
            line_copy(place, chunk, box + 2, own_send.at[0, chunk]).wait_send()

        @pl.when(place > 0)
        def _():
            line_copy(place, chunk, box - 2, own_send.at[1, chunk]).wait_send()

    @pl.when(slab < n_slab - 1)
    def _():
        halo_copy(0).wait_send()

    @pl.when(slab > 0)
    def _():
        halo_copy(1).wait_send()


def on_device(
    n_slab,
    n_box,
    currents,
    aggregate,
    disaggregate,
    trans_table,
    trans_src,
    trans_kind,
    near_blocks,
    near_src,
    near_kind,
):
    n_own, unk, exc = currents.shape
    dirs = aggregate.shape[1]
    n_trans = trans_src.shape[1]
    chips = n_box // 2
    smem = pl.BlockSpec(memory_space=pltpu.SMEM)
    anywhere = pl.BlockSpec(memory_space=pl.ANY)
    dma = pltpu.SemaphoreType.DMA
    return pl.pallas_call(
        functools.partial(kernel, n_slab, n_box),
        out_shape=jax.ShapeDtypeStruct((n_own, unk, exc), jnp.float32),
        in_specs=[smem] * 4 + [anywhere] * 5,
        out_specs=pl.BlockSpec(memory_space=pltpu.VMEM),
        scratch_shapes=[
            pltpu.VMEM((n_box * n_own, unk, exc), jnp.bfloat16),
            pltpu.VMEM((3 * n_own, unk, exc), jnp.bfloat16),
            pltpu.VMEM(aggregate.shape, jnp.bfloat16),
            pltpu.VMEM(disaggregate.shape, jnp.bfloat16),
            pltpu.VMEM((2, unk, dirs), jnp.float32),
            pltpu.VMEM(trans_table.shape, jnp.float32),
            pltpu.VMEM(near_blocks.shape, jnp.bfloat16),
            pltpu.VMEM((n_trans * unk, 2 * dirs), jnp.bfloat16),
            pltpu.VMEM((n_own, 2 * unk, n_trans * unk), jnp.bfloat16),
            dma((6,)),
            dma((2,)),
            dma((2,)),
            dma((2, CHUNKS)),
            dma((chips, CHUNKS)),
            dma((chips, CHUNKS)),
            dma((chips, CHUNKS)),
            dma((chips, CHUNKS)),
        ],
        compiler_params=pltpu.CompilerParams(
            collective_id=0, has_side_effects=True, vmem_limit_bytes=60 * 2**20
        ),
    )(
        trans_src.T,
        trans_kind.T,
        near_src,
        near_kind,
        currents,
        aggregate,
        disaggregate,
        trans_table,
        near_blocks,
    )


def solution(mesh):
    placed = (
        P(("slab", "box"), None, None),
        P(),
        P(),
        P(),
        P("slab", None),
        P("slab", None),
        P(),
        P(("slab", "box"), None),
        P(("slab", "box"), None),
    )
    return jax.shard_map(
        functools.partial(on_device, mesh.shape["slab"], mesh.shape["box"]),
        mesh=mesh,
        in_specs=placed,
        out_specs=P(("slab", "box"), None, None),
        check_vma=False,
    )
```

time: 168 us -> 29.1 us (0.17)
  waiting for transfers between devices: 64.3 us -> 0 us
  other arithmetic: 31.2 us -> 0 us
  local copies, waits for them, and re-layouts: 30.2 us -> 1.87 us
  Pallas kernels: 0 us -> 27 us
  matrix products: 24.8 us -> 0 us
  starting transfers between devices: 15.6 us -> 0 us
    all_to_all x2 -> x0, waiting for transfers between devices: 59.4 us -> none  [the longest x1 33.3 us: on_device(): lax.all_to_all(pattern, 'box', split_axis=2, concat_axis=0, tiled=True)]
    pallas_call x0 -> x1, Pallas kernels: none -> 27 us  [on_device(): pl.pallas_call(functools.partial(kernel, n_slab, n_box), out_shape=jax.Sh...]
    dot_general x5 -> x0, matrix products: 24.8 us -> none  [the longest x1 11.2 us: on_device(): jnp.einsum('bulv,blve->bue', blocks, sources, preferred_element_type=jnp....]
    gather x8 -> x0, local copies, waits for them, and re-layouts: 17.4 us -> none  [the longest x4 9.1 us: translate(): source = pattern[sources[:, entry]].astype(jnp.float32)]
    another operation x3 -> x0, other arithmetic: 15.5 us -> none
    convert_element_type x4 -> x0, other arithmetic: 14.5 us -> none  [translate(): source = pattern[sources[:, entry]].astype(jnp.float32)]
    all_to_all x2 -> x0, starting transfers between devices: 11 us -> none  [the longest x1 6.51 us: on_device(): lax.all_to_all(pattern, 'box', split_axis=2, concat_axis=0, tiled=True)]
    ppermute x2 -> x0, waiting for transfers between devices: 4.92 us -> none  [the longest x1 4.92 us: with_halo(): lax.ppermute(lax.slice_in_dim(block, 0, width, axis=dim), axis, backward)]
  transfers between devices with their start and end apart: 4 -> 0, of which waited for: 3 -> 0; matrix products, arithmetic and copies ran while one was open for 16% -> 0% of each run, Pallas kernels for 0% -> 0%
where the time goes in v1:
time: 29.1 us; the launch traced here: 28.9 us
  Pallas kernels  27 us (93%)
  local copies, waits for them, and re-layouts  1.87 us (6%)
    pallas_call x1, Pallas kernels, on_device(): pl.pallas_call(functools.partial(kernel, n_slab, n_box), out_shape=jax.Sh...  27 us
    unnamed x1, local copies, waits for them, and re-layouts  1.87 us

profile of v1, /device:TPU:1, one launch (start us, length us, event | category | flops | bytes accessed | tf_op | source)
XLA Modules:
  0.0 28.9 jit_solution(4850703674004251499)
XLA Ops:
  0.0 27.0 %shard_map.91 = f32[8,128,128]{2,1,0:T(8,128)} custom-call(s32[4,64]{1,0:T(4,128)} %bitcast.2, s32[4,64]{1,0:T(4,128)} %bitcast.3, s32[8,27]{1,0:T(8,128)} %near_src.1, s32[8,27]{1,0:T(8,128)} %near_kind.1, bf16[8,128,128]{2,1,0:T(8,128)(2,1)} %currents.1, bf16[2,512,128]{2,1,0:T(8,128)(2,1)} %aggregate.1, bf16[128,2,512]{2,1,0:T(2,128)(2,1)} %disaggregate.1, ...), custom_call_target="tpu_custom_call" | custom-call | tf_op jit(solution)/shard_map/pallas_call | solution.py:315
  27.0 1.9 %copy.11 = f32[8,128,128]{2,1,0:T(8,128)} copy(f32[8,128,128]{2,1,0:T(8,128)} %shard_map.91) | data formatting | bytes 1048576

commit v2 on v1

--- a/solution.py
+++ b/solution.py
@@ -52,7 +52,9 @@
     core = box % 2
     chips = n_box // 2
     n_own, unk, exc = currents.shape
-    per = n_own // CHUNKS
+    first = n_own * 3 // 4
+    starts = (0, first)
+    sizes = (first, n_own - first)
     dirs = agg.shape[1]
     n_trans = trans_src.shape[0]
     n_near = near_src.shape[1]
@@ -81,7 +83,7 @@
         pltpu.make_async_copy(aggregate, agg, load_sem.at[4]),
         pltpu.make_async_copy(near_blocks, blocks, load_sem.at[5]),
     ]
-    for load in loads:
+    for load in loads[:2]:
         load.start()
 
     barrier = pltpu.get_barrier_semaphore()
@@ -99,7 +101,7 @@
     pl.semaphore_wait(barrier, met)
 
     def part(origin, lane, chunk):
-        return gathered.at[pl.ds((origin * 2 + lane) * n_own + chunk * per, per)]
+        return gathered.at[pl.ds((origin * 2 + lane) * n_own + starts[chunk], sizes[chunk])]
 
     def line_copy(origin, chunk, target, send):
         return pltpu.make_async_remote_copy(
@@ -141,6 +143,8 @@
         def _():
             line_copy(place, chunk, box - 2, own_send.at[1, chunk]).start()
 
+    for load in loads[2:]:
+        load.start()
     loads[1].wait()
 
     @pl.when(slab < n_slab - 1)
@@ -264,7 +268,8 @@
         for chunk in range(CHUNKS):
             pair_copy(origin, 1 - core, chunk).wait_recv()
 
-    lax.fori_loop(0, n_own, far_unit, 0)
+    for b in range(n_own):
+        far_unit(b, 0)
 
     for origin in range(chips):
         for chunk in range(CHUNKS):

time: 29.1 us -> 28.1 us (0.966)
  Pallas kernels: 27 us -> 26 us
    pallas_call x1, Pallas kernels: 27 us -> 26 us  [on_device(): pl.pallas_call(functools.partial(kernel, n_slab, n_box), out_shape=jax.Sh...]
where the time goes in v2:
time: 28.1 us; the launch traced here: 27.9 us
  Pallas kernels  26 us (93%)
  local copies, waits for them, and re-layouts  1.87 us (7%)
    pallas_call x1, Pallas kernels, on_device(): pl.pallas_call(functools.partial(kernel, n_slab, n_box), out_shape=jax.Sh...  26 us
    unnamed x1, local copies, waits for them, and re-layouts  1.87 us

profile of v2, /device:TPU:1, one launch (start us, length us, event | category | flops | bytes accessed | tf_op | source)
XLA Modules:
  0.0 27.9 jit_solution(945251770772981182)
XLA Ops:
  0.0 26.0 %shard_map.91 = f32[8,128,128]{2,1,0:T(8,128)} custom-call(s32[4,64]{1,0:T(4,128)} %bitcast.2, s32[4,64]{1,0:T(4,128)} %bitcast.3, s32[8,27]{1,0:T(8,128)} %near_src.1, s32[8,27]{1,0:T(8,128)} %near_kind.1, bf16[8,128,128]{2,1,0:T(8,128)(2,1)} %currents.1, bf16[2,512,128]{2,1,0:T(8,128)(2,1)} %aggregate.1, bf16[128,2,512]{2,1,0:T(2,128)(2,1)} %disaggregate.1, ...), custom_call_target="tpu_custom_call" | custom-call | tf_op jit(solution)/shard_map/pallas_call | solution.py:320
  26.0 1.9 %copy.11 = f32[8,128,128]{2,1,0:T(8,128)} copy(f32[8,128,128]{2,1,0:T(8,128)} %shard_map.91) | data formatting | bytes 1048576

commit v3 on v2

--- a/solution.py
+++ b/solution.py
@@ -35,9 +35,11 @@
     dis_wide,
     table,
     blocks,
+    total,
     weights,
     operators,
     load_sem,
+    store_sem,
     halo_send,
     halo_recv,
     own_send,
@@ -205,7 +207,7 @@
     def near_unit(b, carry):
         lhs = jnp.concatenate([blocks[near_kind[b, i]] for i in range(n_near)], axis=1)
         rhs = jnp.concatenate([cand[near_src[b, i]] for i in range(n_near)], axis=0)
-        out[b] = jnp.dot(lhs, rhs, preferred_element_type=jnp.float32)
+        total[b] = jnp.dot(lhs, rhs, preferred_element_type=jnp.float32)
         return carry
 
     def far_unit(b, carry):
@@ -213,7 +215,7 @@
             [gathered[trans_src[i, box * n_own + b]] for i in range(n_trans)], axis=0
         )
         both = jnp.dot(operators[b], rhs, preferred_element_type=jnp.float32)
-        out[b] = out[b] + (both[0:unk] + both[unk:])
+        total[b] = total[b] + (both[0:unk] + both[unk:])
         return carry
 
     def forward(step, chunk):
@@ -270,6 +272,7 @@
 
     for b in range(n_own):
         far_unit(b, 0)
+        pltpu.make_async_copy(total.at[b], out.at[b], store_sem.at[b]).start()
 
     for origin in range(chips):
         for chunk in range(CHUNKS):
@@ -295,6 +298,20 @@
     @pl.when(slab > 0)
     def _():
         halo_copy(1).wait_send()
+
+    for b in range(n_own):
+        pltpu.make_async_copy(total.at[b], out.at[b], store_sem.at[b]).wait()
+
+
+def hand_on(source, out, sem):
+    copies = [
+        pltpu.make_async_copy(source.at[b], out.at[b], sem.at[b])
+        for b in range(source.shape[0])
+    ]
+    for copy in copies:
+        copy.start()
+    for copy in copies:
+        copy.wait()
 
 
 def on_device(
@@ -317,11 +334,11 @@
     smem = pl.BlockSpec(memory_space=pltpu.SMEM)
     anywhere = pl.BlockSpec(memory_space=pl.ANY)
     dma = pltpu.SemaphoreType.DMA
-    return pl.pallas_call(
+    field = pl.pallas_call(
         functools.partial(kernel, n_slab, n_box),
         out_shape=jax.ShapeDtypeStruct((n_own, unk, exc), jnp.float32),
         in_specs=[smem] * 4 + [anywhere] * 5,
-        out_specs=pl.BlockSpec(memory_space=pltpu.VMEM),
+        out_specs=anywhere,
         scratch_shapes=[
             pltpu.VMEM((n_box * n_own, unk, exc), jnp.bfloat16),
             pltpu.VMEM((3 * n_own, unk, exc), jnp.bfloat16),
@@ -330,9 +347,11 @@
             pltpu.VMEM((2, unk, dirs), jnp.float32),
             pltpu.VMEM(trans_table.shape, jnp.float32),
             pltpu.VMEM(near_blocks.shape, jnp.bfloat16),
+            pltpu.VMEM((n_own, unk, exc), jnp.float32),
             pltpu.VMEM((n_trans * unk, 2 * dirs), jnp.bfloat16),
             pltpu.VMEM((n_own, 2 * unk, n_trans * unk), jnp.bfloat16),
             dma((6,)),
+            dma((n_own,)),
             dma((2,)),
             dma((2,)),
             dma((2, CHUNKS)),
@@ -355,6 +374,13 @@
         trans_table,
         near_blocks,
     )
+    return pl.pallas_call(
+        hand_on,
+        out_shape=jax.ShapeDtypeStruct(field.shape, field.dtype),
+        in_specs=[anywhere],
+        out_specs=anywhere,
+        scratch_shapes=[dma((n_own,))],
+    )(field)
 
 
 def solution(mesh):

time: 28.1 us -> 43.1 us (1.53)
  Pallas kernels: 26 us -> 42.9 us
  local copies, waits for them, and re-layouts: 1.87 us -> 0 us
    pallas_call x0 -> x1, Pallas kernels: none -> 17.1 us  [on_device(): pl.pallas_call(hand_on, out_shape=jax.ShapeDtypeStruct(field.shape, field...]
    unnamed x1 -> x0, local copies, waits for them, and re-layouts: 1.87 us -> none
where the time goes in v3:
time: 43.1 us; the launch traced here: 42.9 us
  Pallas kernels  42.9 us (100%)
    pallas_call x1, Pallas kernels, on_device(): pl.pallas_call(functools.partial(kernel, n_slab, n_box), out_shape=jax.Sh...  25.8 us
    pallas_call x1, Pallas kernels, on_device(): pl.pallas_call(hand_on, out_shape=jax.ShapeDtypeStruct(field.shape, field...  17.1 us

profile of v3, /device:TPU:1, one launch (start us, length us, event | category | flops | bytes accessed | tf_op | source)
XLA Modules:
  0.0 42.9 jit_solution(2223601407320904410)
XLA Ops:
  0.0 25.8 %shard_map.91.source = f32[8,128,128]{2,1,0:T(8,128)} custom-call(s32[4,64]{1,0:T(4,128)} %bitcast.2, s32[4,64]{1,0:T(4,128)} %bitcast.3, s32[8,27]{1,0:T(8,128)} %near_src.1, s32[8,27]{1,0:T(8,128)} %near_kind.1, bf16[8,128,128]{2,1,0:T(8,128)(2,1)} %currents.1, bf16[2,512,128]{2,1,0:T(8,128)(2,1)} %aggregate.1, bf16[128,2,512]{2,1,0:T(2,128)(2,1)} %disaggregate.1, ...), custom_call_target="tpu_custom_call" | custom-call | tf_op jit(solution)/shard_map/pallas_call | solution.py:337
  25.8 17.1 %shard_map.92 = f32[8,128,128]{2,1,0:T(8,128)} custom-call(f32[8,128,128]{2,1,0:T(8,128)} %shard_map.91.source), custom_call_target="tpu_custom_call" | custom-call | tf_op jit(solution)/shard_map/pallas_call | solution.py:377

commit v4 on v3

--- a/solution.py
+++ b/solution.py
@@ -303,15 +303,17 @@
         pltpu.make_async_copy(total.at[b], out.at[b], store_sem.at[b]).wait()
 
 
-def hand_on(source, out, sem):
-    copies = [
-        pltpu.make_async_copy(source.at[b], out.at[b], sem.at[b])
-        for b in range(source.shape[0])
-    ]
-    for copy in copies:
-        copy.start()
-    for copy in copies:
-        copy.wait()
+def hand_on(source, out, held, load_sem, store_sem):
+    count = source.shape[0]
+    loads = [pltpu.make_async_copy(source.at[b], held.at[b], load_sem.at[b]) for b in range(count)]
+    stores = [pltpu.make_async_copy(held.at[b], out.at[b], store_sem.at[b]) for b in range(count)]
+    for load in loads:
+        load.start()
+    for load, store in zip(loads, stores):
+        load.wait()
+        store.start()
+    for store in stores:
+        store.wait()
 
 
 def on_device(
@@ -379,7 +381,7 @@
         out_shape=jax.ShapeDtypeStruct(field.shape, field.dtype),
         in_specs=[anywhere],
         out_specs=anywhere,
-        scratch_shapes=[dma((n_own,))],
+        scratch_shapes=[pltpu.VMEM(field.shape, field.dtype), dma((n_own,)), dma((n_own,))],
     )(field)
 
 

time: 43.1 us -> 27.9 us (0.65)
  Pallas kernels: 42.9 us -> 27.7 us
    pallas_call x1, Pallas kernels: 17.1 us -> 1.83 us  [on_device(): pl.pallas_call(hand_on, out_shape=jax.ShapeDtypeStruct(field.shape, field...]
where the time goes in v4:
time: 27.9 us; the launch traced here: 27.7 us
  Pallas kernels  27.7 us (99%)
    pallas_call x1, Pallas kernels, on_device(): pl.pallas_call(functools.partial(kernel, n_slab, n_box), out_shape=jax.Sh...  25.8 us
    pallas_call x1, Pallas kernels, on_device(): pl.pallas_call(hand_on, out_shape=jax.ShapeDtypeStruct(field.shape, field...  1.83 us

profile of v4, /device:TPU:1, one launch (start us, length us, event | category | flops | bytes accessed | tf_op | source)
XLA Modules:
  0.0 27.7 jit_solution(4403069121832195303)
XLA Ops:
  0.0 25.8 %shard_map.91.source = f32[8,128,128]{2,1,0:T(8,128)} custom-call(s32[4,64]{1,0:T(4,128)} %bitcast.2, s32[4,64]{1,0:T(4,128)} %bitcast.3, s32[8,27]{1,0:T(8,128)} %near_src.1, s32[8,27]{1,0:T(8,128)} %near_kind.1, bf16[8,128,128]{2,1,0:T(8,128)(2,1)} %currents.1, bf16[2,512,128]{2,1,0:T(8,128)(2,1)} %aggregate.1, bf16[128,2,512]{2,1,0:T(2,128)(2,1)} %disaggregate.1, ...), custom_call_target="tpu_custom_call" | custom-call | tf_op jit(solution)/shard_map/pallas_call | solution.py:339
  25.8 1.8 %shard_map.92 = f32[8,128,128]{2,1,0:T(8,128)} custom-call(f32[8,128,128]{2,1,0:T(8,128)} %shard_map.91.source), custom_call_target="tpu_custom_call" | custom-call | tf_op jit(solution)/shard_map/pallas_call | solution.py:379
